TPU v7x, 256 devices: a whole 4x4x8 slice. The times are simulated.
256 devices in a mesh: dp: 16 (over y_lo, z), seq: 16 (over x, y_hi, core).
Axes of the slice: x: 4, y: 4 (y_hi: 2, y_lo: 2; y = y_hi * 2 + y_lo), z: 8, core: 2. Of those that a mesh axis runs over, the one named last changes fastest.
Arguments:
- seq_embed: bfloat16 [16, 3072, 1536], P('dp', 'seq'), may hold values from -24 to 24
- w_qkv: bfloat16 [1536, 2304], P('seq'), may hold values from -1 to 1
- upstream: bfloat16 [16, 3072, 768], P('dp', 'seq'), may hold values from -6 to 6
Outputs:
- attended: bfloat16 [16, 3072, 768], P('dp', 'seq')
- grad_input: bfloat16 [16, 3072, 1536], P('dp', 'seq')
- grad_qkv: bfloat16 [1536, 2304], P('seq')
All inputs are finite; a program needn't handle non-finite values.
Results may differ from a plain program's by a relative error of at most 0.04.
Values may be sent and summed in bfloat16 or wider, within the bound.
A program may use at most 128 MiB of HBM per device.

v0:
```python
import math
import jax
import jax.numpy as jnp
from jax import lax
from jax.sharding import PartitionSpec as P

HEADS = 6


def split_heads(block, heads):
    return block.reshape(block.shape[0], heads, block.shape[1] // heads)


def on_device(seq_embed, w_qkv, upstream):
    heads = HEADS
    width = upstream.shape[-1]
    head_dim = width // heads
    score_scale = 1.0 / math.sqrt(head_dim)
    weights = lax.all_gather(w_qkv, "seq", axis=0, tiled=True)
    tokens = seq_embed[0]
    grad_out = upstream[0]
    rows_here = tokens.shape[0]
    projected = jnp.dot(tokens, weights, preferred_element_type=jnp.float32).astype(jnp.bfloat16)
    queries = projected[:, :width]
    keys_here = projected[:, width : 2 * width]
    values_here = projected[:, 2 * width :]
    keys_all, values_all = (
        lax.all_gather(keys_here, "seq", axis=0, tiled=True),
        lax.all_gather(values_here, "seq", axis=0, tiled=True),
    )
    query_heads = split_heads(queries, heads)
    key_heads = split_heads(keys_all, heads)
    value_heads = split_heads(values_all, heads)
    scores = (
        jnp.einsum("qhd,khd->hqk", query_heads, key_heads, preferred_element_type=jnp.float32)
        * score_scale
    )
    peak = jnp.max(scores, axis=-1, keepdims=True)
    log_total = peak[..., 0] + jnp.log(jnp.sum(jnp.exp(scores - peak), axis=-1))
    probs = jnp.exp(scores - log_total[..., None])
    probs_low = probs.astype(jnp.bfloat16)
    attended_heads = jnp.einsum(
        "hqk,khd->qhd", probs_low, value_heads, preferred_element_type=jnp.float32
    ).astype(jnp.bfloat16)
    grad_heads = split_heads(grad_out, heads)
    delta_rows = jnp.sum(
        grad_heads.astype(jnp.float32) * attended_heads.astype(jnp.float32), axis=-1
    )
    grad_probs = jnp.einsum(
        "qhd,khd->hqk", grad_heads, value_heads, preferred_element_type=jnp.float32
    )
    grad_scores = (probs * (grad_probs - delta_rows.T[..., None]) * score_scale).astype(
        jnp.bfloat16
    )
    grad_queries = jnp.einsum(
        "hqk,khd->qhd", grad_scores, key_heads, preferred_element_type=jnp.float32
    ).astype(jnp.bfloat16)
    lse_all, delta_all = (
        lax.all_gather(log_total.T, "seq", axis=0, tiled=True),
        lax.all_gather(delta_rows, "seq", axis=0, tiled=True),
    )
    key_local = split_heads(keys_here, heads)
    value_local = split_heads(values_here, heads)
    query_piece = split_heads(lax.all_gather(queries, "seq", axis=0, tiled=True), heads)
    grad_piece = split_heads(lax.all_gather(grad_out, "seq", axis=0, tiled=True), heads)
    lse_piece = lse_all.T
    delta_piece = delta_all.T
    piece_scores = (
        jnp.einsum("qhd,khd->hqk", query_piece, key_local, preferred_element_type=jnp.float32)
        * score_scale
    )
    piece_probs = jnp.exp(piece_scores - lse_piece[..., None])
    grad_values = jnp.einsum(
        "hqk,qhd->khd",
        piece_probs.astype(jnp.bfloat16),
        grad_piece,
        preferred_element_type=jnp.float32,
    )
    piece_grad_probs = jnp.einsum(
        "qhd,khd->hqk", grad_piece, value_local, preferred_element_type=jnp.float32
    )
    piece_grad_scores = (
        piece_probs * (piece_grad_probs - delta_piece[..., None]) * score_scale
    ).astype(jnp.bfloat16)
    grad_keys = jnp.einsum(
        "hqk,qhd->khd", piece_grad_scores, query_piece, preferred_element_type=jnp.float32
    )
    grad_keys, grad_values = (grad_keys, grad_values)
    grad_proj = jnp.concatenate(
        [
            grad_queries.reshape(rows_here, width),
            grad_keys.astype(jnp.bfloat16).reshape(rows_here, width),
            grad_values.astype(jnp.bfloat16).reshape(rows_here, width),
        ],
        axis=1,
    )
    grad_input = lax.dot_general(
        grad_proj, weights, (((1,), (1,)), ((), ())), preferred_element_type=jnp.float32
    ).astype(jnp.bfloat16)
    term = lax.dot_general(
        tokens, grad_proj, (((0,), (0,)), ((), ())), preferred_element_type=jnp.float32
    )
    summed = lax.psum_scatter(
        lax.optimization_barrier(term.astype(jnp.bfloat16))
        .astype(jnp.float32)
        .astype(jnp.bfloat16),
        "seq",
        scatter_dimension=0,
        tiled=True,
    )
    total = lax.psum(summed, "dp").astype(jnp.float32)
    attended = attended_heads.reshape(rows_here, width)
    return (attended[None], grad_input[None], total.astype(jnp.bfloat16))


def solution(mesh):
    placed = (P("dp", "seq", None), P("seq", None), P("dp", "seq", None))
    return jax.shard_map(
        on_device,
        mesh=mesh,
        in_specs=placed,
        out_specs=(P("dp", "seq", None), P("dp", "seq", None), P("seq", None)),
        check_vma=False,
    )
```

profile of v0, /device:TPU:2, one launch (start us, length us, event | category | flops | bytes accessed | tf_op | source)
XLA Modules:
  0.0 663.6 jit_solution(6117910122317396261)
XLA Ops:
  7.2 0.7 all-gather.9.cloned.1.call-update
  8.0 0.7 all-gather.17.cloned.1.call-update
  8.7 76.5 %all-gather.9.cloned.1.call-done = bf16[1536,2304]{1,0:T(8,128)(2,1)} async-done(((bf16[96,2304]{1,0:T(8,128)(2,1)}), bf16[1536,2304]{1,0:T(8,128)(2,1)}) %all-gather.9.cloned.1.call-update) | async-done | bytes 7077904 | tf_op jit(solution)/shard_map/all_gather | solution.py:19
  85.2 4.5 convolution_convert_fusion.1
  89.7 1.0 slice_bitcast_fusion.2
  90.8 0.5 all-gather.13.cloned.1.call-update
  91.4 0.5 all-gather.15.cloned.1.call-update
  92.3 57.5 %all-gather.17.cloned.1.call-done = bf16[1,3072,768]{2,1,0:T(8,128)(2,1)} async-done(((bf16[1,192,768]{2,1,0:T(8,128)(2,1)}), bf16[1,3072,768]{2,1,0:T(8,128)(2,1)}) %all-gather.17.cloned.1.call-update) | async-done | bytes 4718608 | tf_op jit(solution)/shard_map/all_gather | solution.py:65
  149.8 6.7 %copy.47 = bf16[1,3072,768]{1,2,0:T(8,128)(2,1)} copy(bf16[1,3072,768]{2,1,0:T(8,128)(2,1)} %all-gather.17.cloned.1.call-done) | data formatting | bytes 9437184 | tf_op jit(solution)/shard_map/all_gather | solution.py:65
  156.5 58.5 %all-gather.11.cloned.1.call-done = bf16[3072,768]{1,0:T(8,128)(2,1)} async-done(((bf16[192,768]{1,0:T(8,128)(2,1)}), bf16[3072,768]{1,0:T(8,128)(2,1)}) %all-gather.11.cloned.1.call-update) | async-done | bytes 4718608 | tf_op jit(solution)/shard_map/all_gather | solution.py:29
  215.0 6.7 %copy.32 = bf16[3072,768]{0,1:T(8,128)(2,1)} copy(bf16[3072,768]{1,0:T(8,128)(2,1)} %all-gather.11.cloned.1.call-done) | data formatting | bytes 9437184 | tf_op jit(solution)/shard_map/all_gather | solution.py:29
  221.7 58.3 %all-gather.13.cloned.1.call-done = bf16[3072,768]{1,0:T(8,128)(2,1)} async-done(((bf16[192,768]{1,0:T(8,128)(2,1)}), bf16[3072,768]{1,0:T(8,128)(2,1)}) %all-gather.13.cloned.1.call-update) | async-done | bytes 4718608 | tf_op jit(solution)/shard_map/all_gather | solution.py:28
  280.0 6.7 %copy.33 = bf16[3072,768]{0,1:T(8,128)(2,1)} copy(bf16[3072,768]{1,0:T(8,128)(2,1)} %all-gather.13.cloned.1.call-done) | data formatting | bytes 9437184 | tf_op jit(solution)/shard_map/all_gather | solution.py:28
  286.7 9.6 %multiply_reduce_fusion = (f32[6,192]{1,0:T(8,128)S(1)}, f32[6,192,3072]{2,1,0:T(8,128)}) fusion(bf16[3072,6,128]{0,2,1:T(8,128)(2,1)} %bitcast.94, bf16[24,6,8,128]{3,2,1,0:T(8,128)(2,1)S(1)} %get-tuple-element.13), kind=kOutput, calls=%fused_computation.11 | convolution fusion | flops 913046400 | bytes 19173888 | tf_op jit(solution)/shard_map/qhd,khd->hqk/dot_general | solution.py:35
  296.3 7.5 %exponential_reduce_fusion = f32[6,192]{1,0:T(8,128)S(1)} fusion(f32[6,192,3072]{2,1,0:T(8,128)} %get-tuple-element.19, f32[6,192]{1,0:T(8,128)S(1)} %get-tuple-element.18), kind=kLoop, calls=%fused_computation.8 | loop fusion | flops 10615680 | bytes 14164992 | tf_op jit(solution)/shard_map/reduce_sum | solution.py:39
  303.8 8.5 %multiply_reduce_fusion.1 = (f32[192,6]{0,1:T(8,128)S(1)}, bf16[192,6,128]{2,0,1:T(8,128)(2,1)}) fusion(bf16[192,6,128]{2,1,0:T(8,128)(2,1)S(1)} %reshape_squeeze.3, bf16[3072,6,128]{0,2,1:T(8,128)(2,1)S(1)} %bitcast.103, f32[6,192,3072]{2,1,0:T(8,128)} %get-tuple-element.19, f32[6,192]{1,0:T(8,128)S(1)} %log_add_fusion), kind=kOutput, calls=%fused_computation.37 | convolution fusion | flops 917322624 | bytes 19473408 | tf_op jit(solution)/shard_map/hqk,khd->qhd/dot_general | solution.py:42
  312.3 20.3 %all-gather.2 = f32[16,192,6]{1,2,0:T(8,128)S(1)} all-gather(f32[1,192,6]{1,2,0:T(8,128)S(1)} %bitcast.108), channel_id=1, replica_groups=mesh['dp'=16,'seq'=16] {'seq'}, dimensions={0}, use_global_device_ids=true | all-gather | bytes 78336 | tf_op jit(solution)/shard_map/all_gather | solution.py:60
  332.8 20.5 %all-gather.1 = f32[16,192,6]{1,2,0:T(8,128)S(1)} all-gather(f32[1,192,6]{1,2,0:T(8,128)S(1)} %bitcast.107), channel_id=1, replica_groups=mesh['dp'=16,'seq'=16] {'seq'}, dimensions={0}, use_global_device_ids=true | all-gather | bytes 78336 | tf_op jit(solution)/shard_map/all_gather | solution.py:59
  353.5 10.7 %fusion.42 = bf16[6,24,8,128]{3,2,1,0:T(8,128)(2,1)S(1)} fusion(bf16[3072,6,128]{0,2,1:T(8,128)(2,1)} %bitcast.95, f32[6,192,3072]{2,1,0:T(8,128)} %get-tuple-element.19, f32[6,192]{1,0:T(8,128)S(1)} %bitcast.109, f32[6,192]{1,0:T(8,128)S(1)} %log_add_fusion, bf16[3072,6,128]{0,2,1:T(8,128)(2,1)} %bitcast.100, bf16[192,6,128]{2,1,0:T(8,128)(2,1)S(1)} %reshape_squeeze.3), kind=kOutput, calls=%fused_computation.33 | convolution fusion | flops 1833320448 | bytes 24192000 | tf_op jit(solution)/shard_map/hqk,khd->qhd/dot_general | solution.py:55
  364.3 6.7 %copy.43 = bf16[3072,768]{0,1:T(8,128)(2,1)} copy(bf16[3072,768]{1,0:T(8,128)(2,1)} %all-gather.15.cloned.1.call-done) | data formatting | bytes 9437184 | tf_op jit(solution)/shard_map/all_gather | solution.py:64
  371.0 9.4 %fusion.54 = f32[6,3072,192]{1,2,0:T(8,128)} fusion(bf16[3072,6,128]{0,2,1:T(8,128)(2,1)} %bitcast.96, bf16[24,6,8,128]{3,2,1,0:T(8,128)(2,1)S(1)} %get-tuple-element.14), kind=kOutput, calls=%fused_computation.43 | convolution fusion | flops 905969664 | bytes 19169280 | tf_op jit(solution)/shard_map/qhd,khd->hqk/dot_general | solution.py:69
  380.3 8.8 %fusion.36 = bf16[6,24,8,128]{3,2,1,0:T(8,128)(2,1)S(1)} fusion(bf16[3072,6,128]{0,2,1:T(8,128)(2,1)} %bitcast.98, f32[6,3072,192]{1,2,0:T(8,128)} %fusion.54, f32[6,3072]{1,0:T(8,128)S(1)} %bitcast.105), kind=kOutput, calls=%fused_computation.31 | convolution fusion | flops 916733952 | bytes 19243008 | tf_op jit(solution)/shard_map/hqk,qhd->khd/dot_general | solution.py:73
  389.1 10.9 %fusion.45 = bf16[6,24,8,128]{3,2,1,0:T(8,128)(2,1)S(1)} fusion(bf16[3072,6,128]{0,2,1:T(8,128)(2,1)} %bitcast.97, f32[6,3072,192]{1,2,0:T(8,128)} %fusion.54, f32[6,3072]{1,0:T(8,128)S(1)} %bitcast.104, f32[6,3072]{1,0:T(8,128)} %bitcast.106, bf16[3072,6,128]{0,2,1:T(8,128)(2,1)} %bitcast.99, bf16[24,6,8,128]{3,2,1,0:T(8,128)(2,1)S(1)} %get-tuple-element.12), kind=kOutput, calls=%fused_computation.34 | convolution fusion | flops 1833320448 | bytes 24330240 | tf_op jit(solution)/shard_map/hqk,qhd->khd/dot_general | solution.py:85
  400.1 5.0 fusion.6
  405.1 9.8 %copy.64 = bf16[1536,2304]{1,0:T(8,128)(2,1)} copy(bf16[1536,2304]{0,1:T(8,128)(2,1)} %fusion.6) | data formatting | bytes 14155776
  415.0 0.9 copy-done.2
  416.1 1.1 broadcast_in_dim_reshape.3
  417.1 99.5 %reduce-scatter.4.cloned.1.call-done = bf16[96,2304]{1,0:T(8,128)(2,1)} async-done(((bf16[1536,2304]{1,0:T(8,128)(2,1)}), bf16[96,2304]{1,0:T(8,128)(2,1)}) %reduce-scatter.4.cloned.1.call-update) | async-done | bytes 442384
  516.7 2.1 copy.65
  518.8 6.3 fusion.23
  525.0 129.7 %all-reduce.2.cloned.1.call-done = bf16[96,2304]{0,1:T(8,128)(2,1)} async-done(((bf16[96,2304]{0,1:T(8,128)(2,1)}), bf16[96,2304]{0,1:T(8,128)(2,1)}) %all-reduce.2.cloned.1.call-update) | async-done | bytes 442384 | tf_op jit(solution)/shard_map/psum | solution.py:111
  654.7 2.1 copy.55
  (33 shorter events, 1.3 us)
Async XLA Ops:
  7.2 78.0 %copy-start = (bf16[1,192,1536]{2,1,0:T(8,128)(2,1)S(1)}, bf16[1,192,1536]{2,1,0:T(8,128)(2,1)}, u32[]{:S(2)}) copy-start(bf16[1,192,1536]{2,1,0:T(8,128)(2,1)} %param.3) | copy-start | bytes 1769476
  7.2 78.0 %all-gather.9.cloned.1.call-start = ((), (), s32[]{:S(2)}) async-start(), calls=%async_computation.1 | async-start | bytes 7520256 | tf_op jit(solution)/shard_map/all_gather | solution.py:19
  7.9 141.9 %all-gather.17.cloned.1.call-start = ((), (), s32[]{:S(2)}) async-start(), calls=%async_computation.6 | async-start | bytes 5013504 | tf_op jit(solution)/shard_map/all_gather | solution.py:65
  8.7 83.3 %copy-start.1 = (bf16[1,192,768]{2,1,0:T(8,128)(2,1)S(1)}, bf16[1,192,768]{2,1,0:T(8,128)(2,1)}, u32[]{:S(2)}) copy-start(bf16[1,192,768]{2,1,0:T(8,128)(2,1)} %param.5) | copy-start | bytes 884740
  8.7 206.3 %all-gather.11.cloned.1.call-start = ((), (), s32[]{:S(2)}) async-start(), calls=%async_computation.2 | async-start | bytes 5013504 | tf_op jit(solution)/shard_map/all_gather | solution.py:29
  90.8 189.2 %all-gather.13.cloned.1.call-start = ((), (), s32[]{:S(2)}) async-start(), calls=%async_computation.3 | async-start | bytes 5013504 | tf_op jit(solution)/shard_map/all_gather | solution.py:28
  91.3 272.9 %all-gather.15.cloned.1.call-start = ((), (), s32[]{:S(2)}) async-start(), calls=%async_computation.4 | async-start | bytes 5013504 | tf_op jit(solution)/shard_map/all_gather | solution.py:64
  91.9 424.7 %reduce-scatter.4.cloned.1.call-start = ((), (), s32[]{:S(2)}) async-start(), calls=%async_computation.7 | async-start | bytes 7520256
  280.0 23.8 %slice-start = ((s8[4718592]{0:T(1024)(128)(4,1)}), s8[524288]{0:T(1024)(128)(4,1)S(1)}, s32[]{:S(2)}) async-start(s8[4718592]{0:T(1024)(128)(4,1)} %bitcast.101), calls=%async_computation.8 | async-start | bytes 1048576
  286.7 17.1 %slice-start.1 = ((s8[4718592]{0:T(1024)(128)(4,1)}), s8[4194304]{0:T(1024)(128)(4,1)S(1)}, s32[]{:S(2)}) async-start(s8[4718592]{0:T(1024)(128)(4,1)} %bitcast.101), calls=%async_computation.9 | async-start | bytes 8388608
  353.5 26.9 %copy-start.3 = (f32[3072,6]{0,1:T(8,128)}, f32[3072,6]{0,1:T(8,128)S(1)}, u32[]{:S(2)}) copy-start(f32[3072,6]{0,1:T(8,128)S(1)} %reshape.59) | copy-start | bytes 221188
  414.9 1.0 copy-start.2
  414.9 239.8 %all-reduce.2.cloned.1.call-start = ((), (), s32[]{:S(2)}) async-start(), calls=%async_computation.5 | async-start | bytes 1179648 | tf_op jit(solution)/shard_map/psum | solution.py:111
Sparse Core Ops, SparseCore 0:
  10.7 74.4 all-gather.8
  87.9 61.8 all-gather.16
  153.1 61.8 all-gather.10
  218.1 61.8 all-gather.12
  283.1 62.3 all-gather.14
  415.0 101.5 reduce-scatter.3
  519.3 135.3 all-reduce.1
where the time goes:
time: 665 us; the launch traced here: 664 us
  waiting for transfers between devices  482 us (72%)
  matrix products  73.6 us (11%)
  local copies, waits for them, and re-layouts  44.6 us (7%)
  blocking collectives  40.9 us (6%)
  between operations  14.3 us (2%)
  other arithmetic  7.47 us (1%)
    psum x1, waiting for transfers between devices, on_device(): total = lax.psum(summed, 'dp').astype(jnp.float32)  130 us
    unnamed x8, waiting for transfers between devices  102 us
    all_gather x1, waiting for transfers between devices, on_device(): weights = lax.all_gather(w_qkv, 'seq', axis=0, tiled=True)  76.5 us
    all_gather x1, waiting for transfers between devices, on_device(): lax.all_gather(values_here, 'seq', axis=0, tiled=True)  58.5 us
    all_gather x1, waiting for transfers between devices, on_device(): lax.all_gather(keys_here, 'seq', axis=0, tiled=True)  58.3 us
    all_gather x1, waiting for transfers between devices, on_device(): lax.all_gather(grad_out, 'seq', axis=0, tiled=True)  57.5 us
    all_gather x1, blocking collectives, on_device(): lax.all_gather(log_total.T, 'seq', axis=0, tiled=True)  20.5 us
    all_gather x1, blocking collectives, on_device(): lax.all_gather(delta_rows, 'seq', axis=0, tiled=True)  20.3 us
  transfers between devices with their start and end apart: 7, of which 6 were waited for; matrix products, arithmetic and copies ran while one was open for 11% of the time, Pallas kernels for 0%

commit v1 on v0

--- a/solution.py
+++ b/solution.py
@@ -16,7 +16,8 @@
     width = upstream.shape[-1]
     head_dim = width // heads
     score_scale = 1.0 / math.sqrt(head_dim)
-    weights = lax.all_gather(w_qkv, "seq", axis=0, tiled=True)
+    sent = jnp.stack([w_qkv] * lax.axis_size("seq"))
+    weights = jnp.concatenate(lax.all_to_all(sent, "seq", 0, 0), axis=0)
     tokens = seq_embed[0]
     grad_out = upstream[0]
     rows_here = tokens.shape[0]

time: 665 us -> 638 us (0.959)
  waiting for transfers between devices: 482 us -> 359 us
  blocking collectives: 40.9 us -> 138 us
    all_to_all x0 -> x1, blocking collectives: none -> 96.8 us  [on_device(): weights = jnp.concatenate(lax.all_to_all(sent, 'seq', 0, 0), axis=0)]
    all_gather x1 -> x0, waiting for transfers between devices: 76.5 us -> none  [on_device(): weights = lax.all_gather(w_qkv, 'seq', axis=0, tiled=True)]
    all_gather x1, waiting for transfers between devices: 57.5 us -> 10.3 us  [on_device(): lax.all_gather(grad_out, 'seq', axis=0, tiled=True)]
    unnamed x20 -> x22, local copies, waits for them, and re-layouts: 16.1 us -> 17.5 us
    unnamed x8 -> x7, waiting for transfers between devices: 102 us -> 101 us
  transfers between devices with their start and end apart: 7 -> 6, of which waited for: 6 -> 5; matrix products, arithmetic and copies ran while one was open for 11% -> 11% of each run, Pallas kernels for 0% -> 0%
where the time goes in v1:
time: 638 us; the launch traced here: 637 us
  waiting for transfers between devices  359 us (56%)
  blocking collectives  138 us (22%)
  matrix products  70.6 us (11%)
  local copies, waits for them, and re-layouts  47.7 us (7%)
  between operations  14.3 us (2%)
  other arithmetic  7.47 us (1%)
    psum x1, waiting for transfers between devices, on_device(): total = lax.psum(summed, 'dp').astype(jnp.float32)  130 us
    unnamed x7, waiting for transfers between devices  101 us
    all_to_all x1, blocking collectives, on_device(): weights = jnp.concatenate(lax.all_to_all(sent, 'seq', 0, 0), axis=0)  96.8 us
    all_gather x1, waiting for transfers between devices, on_device(): lax.all_gather(values_here, 'seq', axis=0, tiled=True)  59.4 us
    all_gather x1, waiting for transfers between devices, on_device(): lax.all_gather(keys_here, 'seq', axis=0, tiled=True)  58.5 us
    all_gather x1, blocking collectives, on_device(): lax.all_gather(log_total.T, 'seq', axis=0, tiled=True)  20.5 us
    all_gather x1, blocking collectives, on_device(): lax.all_gather(delta_rows, 'seq', axis=0, tiled=True)  20.4 us
    unnamed x22, local copies, waits for them, and re-layouts  17.5 us
  transfers between devices with their start and end apart: 6, of which 5 were waited for; matrix products, arithmetic and copies ran while one was open for 11% of the time, Pallas kernels for 0%

profile of v1, /device:TPU:2, one launch (start us, length us, event | category | flops | bytes accessed | tf_op | source)
XLA Modules:
  0.0 637.1 jit_solution(16806106186365798912)
XLA Ops:
  7.2 0.7 all-gather.14.cloned.1.call-update
  8.0 1.7 stack.2
  9.7 96.8 %all_to_all.5 = bf16[16,96,2304]{2,1,0:T(8,128)(2,1)S(1)} all-to-all(bf16[16,96,2304]{2,1,0:T(8,128)(2,1)S(1)} %stack.2), channel_id=1, replica_groups=mesh['dp'=16,'seq'=16] {'seq'}, dimensions={0} | all-to-all | bytes 14155776 | tf_op jit(solution)/shard_map/all_to_all | solution.py:20
  106.5 1.5 convolution_convert_fusion.1
  108.1 1.3 copy-done.1
  109.3 1.0 slice_bitcast_fusion.2
  110.4 0.7 all-gather.10.cloned.1.call-update
  112.1 10.3 %all-gather.14.cloned.1.call-done = bf16[1,3072,768]{2,1,0:T(8,128)(2,1)} async-done(((bf16[1,192,768]{2,1,0:T(8,128)(2,1)}), bf16[1,3072,768]{2,1,0:T(8,128)(2,1)}) %all-gather.14.cloned.1.call-update) | async-done | bytes 4718608 | tf_op jit(solution)/shard_map/all_gather | solution.py:66
  122.3 6.7 %copy.47 = bf16[1,3072,768]{1,2,0:T(8,128)(2,1)} copy(bf16[1,3072,768]{2,1,0:T(8,128)(2,1)} %all-gather.14.cloned.1.call-done) | data formatting | bytes 9437184 | tf_op jit(solution)/shard_map/all_gather | solution.py:66
  129.0 59.4 %all-gather.8.cloned.1.call-done = bf16[3072,768]{1,0:T(8,128)(2,1)} async-done(((bf16[192,768]{1,0:T(8,128)(2,1)}), bf16[3072,768]{1,0:T(8,128)(2,1)}) %all-gather.8.cloned.1.call-update) | async-done | bytes 4718608 | tf_op jit(solution)/shard_map/all_gather | solution.py:30
  188.5 6.7 %copy.32 = bf16[3072,768]{0,1:T(8,128)(2,1)} copy(bf16[3072,768]{1,0:T(8,128)(2,1)} %all-gather.8.cloned.1.call-done) | data formatting | bytes 9437184 | tf_op jit(solution)/shard_map/all_gather | solution.py:30
  195.2 58.5 %all-gather.10.cloned.1.call-done = bf16[3072,768]{1,0:T(8,128)(2,1)} async-done(((bf16[192,768]{1,0:T(8,128)(2,1)}), bf16[3072,768]{1,0:T(8,128)(2,1)}) %all-gather.10.cloned.1.call-update) | async-done | bytes 4718608 | tf_op jit(solution)/shard_map/all_gather | solution.py:29
  253.7 6.7 %copy.33 = bf16[3072,768]{0,1:T(8,128)(2,1)} copy(bf16[3072,768]{1,0:T(8,128)(2,1)} %all-gather.10.cloned.1.call-done) | data formatting | bytes 9437184 | tf_op jit(solution)/shard_map/all_gather | solution.py:29
  260.4 9.6 %multiply_reduce_fusion = (f32[6,192]{1,0:T(8,128)S(1)}, f32[6,192,3072]{2,1,0:T(8,128)}) fusion(bf16[3072,6,128]{0,2,1:T(8,128)(2,1)} %bitcast.95, bf16[24,6,8,128]{3,2,1,0:T(8,128)(2,1)S(1)} %get-tuple-element.13), kind=kOutput, calls=%fused_computation.11 | convolution fusion | flops 913046400 | bytes 19173888 | tf_op jit(solution)/shard_map/qhd,khd->hqk/dot_general | solution.py:36
  270.0 7.5 %exponential_reduce_fusion = f32[6,192]{1,0:T(8,128)S(1)} fusion(f32[6,192,3072]{2,1,0:T(8,128)} %get-tuple-element.19, f32[6,192]{1,0:T(8,128)S(1)} %get-tuple-element.18), kind=kLoop, calls=%fused_computation.8 | loop fusion | flops 10615680 | bytes 14164992 | tf_op jit(solution)/shard_map/reduce_sum | solution.py:40
  277.5 8.5 %multiply_reduce_fusion.1 = (f32[192,6]{0,1:T(8,128)S(1)}, bf16[192,6,128]{2,0,1:T(8,128)(2,1)}) fusion(bf16[192,6,128]{2,1,0:T(8,128)(2,1)S(1)} %reshape_squeeze.3, bf16[3072,6,128]{0,2,1:T(8,128)(2,1)S(1)} %bitcast.106, f32[6,192,3072]{2,1,0:T(8,128)} %get-tuple-element.19, f32[6,192]{1,0:T(8,128)S(1)} %log_add_fusion), kind=kOutput, calls=%fused_computation.37 | convolution fusion | flops 917322624 | bytes 19473408 | tf_op jit(solution)/shard_map/hqk,khd->qhd/dot_general | solution.py:43
  286.0 20.4 %all-gather.2 = f32[16,192,6]{1,2,0:T(8,128)S(1)} all-gather(f32[1,192,6]{1,2,0:T(8,128)S(1)} %bitcast.111), channel_id=1, replica_groups=mesh['dp'=16,'seq'=16] {'seq'}, dimensions={0}, use_global_device_ids=true | all-gather | bytes 78336 | tf_op jit(solution)/shard_map/all_gather | solution.py:61
  306.5 20.5 %all-gather.1 = f32[16,192,6]{1,2,0:T(8,128)S(1)} all-gather(f32[1,192,6]{1,2,0:T(8,128)S(1)} %bitcast.110), channel_id=1, replica_groups=mesh['dp'=16,'seq'=16] {'seq'}, dimensions={0}, use_global_device_ids=true | all-gather | bytes 78336 | tf_op jit(solution)/shard_map/all_gather | solution.py:60
  327.1 10.7 %fusion.42 = bf16[6,24,8,128]{3,2,1,0:T(8,128)(2,1)S(1)} fusion(bf16[3072,6,128]{0,2,1:T(8,128)(2,1)} %bitcast.96, f32[6,192,3072]{2,1,0:T(8,128)} %get-tuple-element.19, f32[6,192]{1,0:T(8,128)S(1)} %bitcast.112, f32[6,192]{1,0:T(8,128)S(1)} %log_add_fusion, bf16[3072,6,128]{0,2,1:T(8,128)(2,1)} %bitcast.103, bf16[192,6,128]{2,1,0:T(8,128)(2,1)S(1)} %reshape_squeeze.3), kind=kOutput, calls=%fused_computation.33 | convolution fusion | flops 1833320448 | bytes 24192000 | tf_op jit(solution)/shard_map/hqk,khd->qhd/dot_general | solution.py:56
  337.9 6.7 %copy.43 = bf16[3072,768]{0,1:T(8,128)(2,1)} copy(bf16[3072,768]{1,0:T(8,128)(2,1)} %all-gather.12.cloned.1.call-done) | data formatting | bytes 9437184 | tf_op jit(solution)/shard_map/all_gather | solution.py:65
  344.6 9.4 %fusion.54 = f32[6,3072,192]{1,2,0:T(8,128)} fusion(bf16[3072,6,128]{0,2,1:T(8,128)(2,1)} %bitcast.97, bf16[24,6,8,128]{3,2,1,0:T(8,128)(2,1)S(1)} %get-tuple-element.14), kind=kOutput, calls=%fused_computation.43 | convolution fusion | flops 905969664 | bytes 19169280 | tf_op jit(solution)/shard_map/qhd,khd->hqk/dot_general | solution.py:70
  354.0 8.8 %fusion.36 = bf16[6,24,8,128]{3,2,1,0:T(8,128)(2,1)S(1)} fusion(bf16[3072,6,128]{0,2,1:T(8,128)(2,1)} %bitcast.101, f32[6,3072,192]{1,2,0:T(8,128)} %fusion.54, f32[6,3072]{1,0:T(8,128)S(1)} %bitcast.108), kind=kOutput, calls=%fused_computation.31 | convolution fusion | flops 916733952 | bytes 19243008 | tf_op jit(solution)/shard_map/hqk,qhd->khd/dot_general | solution.py:74
  362.7 10.9 %fusion.45 = bf16[6,24,8,128]{3,2,1,0:T(8,128)(2,1)S(1)} fusion(bf16[3072,6,128]{0,2,1:T(8,128)(2,1)} %bitcast.98, f32[6,3072,192]{1,2,0:T(8,128)} %fusion.54, f32[6,3072]{1,0:T(8,128)S(1)} %bitcast.107, f32[6,3072]{1,0:T(8,128)} %bitcast.109, bf16[3072,6,128]{0,2,1:T(8,128)(2,1)} %bitcast.102, bf16[24,6,8,128]{3,2,1,0:T(8,128)(2,1)S(1)} %get-tuple-element.12), kind=kOutput, calls=%fused_computation.34 | convolution fusion | flops 1833320448 | bytes 24330240 | tf_op jit(solution)/shard_map/hqk,qhd->khd/dot_general | solution.py:86
  373.7 5.0 fusion.6
  378.7 9.9 %copy.64 = bf16[1536,2304]{1,0:T(8,128)(2,1)} copy(bf16[1536,2304]{0,1:T(8,128)(2,1)} %fusion.6) | data formatting | bytes 14155776
  388.7 0.9 copy-done.3
  389.8 1.1 broadcast_in_dim_reshape.3
  390.9 99.4 %reduce-scatter.4.cloned.1.call-done = bf16[96,2304]{1,0:T(8,128)(2,1)} async-done(((bf16[1536,2304]{1,0:T(8,128)(2,1)}), bf16[96,2304]{1,0:T(8,128)(2,1)}) %reduce-scatter.4.cloned.1.call-update) | async-done | bytes 442384
  490.3 2.1 copy.65
  492.4 6.3 fusion.23
  498.6 129.5 %all-reduce.2.cloned.1.call-done = bf16[96,2304]{0,1:T(8,128)(2,1)} async-done(((bf16[96,2304]{0,1:T(8,128)(2,1)}), bf16[96,2304]{0,1:T(8,128)(2,1)}) %all-reduce.2.cloned.1.call-update) | async-done | bytes 442384 | tf_op jit(solution)/shard_map/psum | solution.py:112
  628.1 2.1 copy.55
  (34 shorter events, 1.8 us)
Async XLA Ops:
  7.2 99.3 %copy-start = (bf16[1,192,1536]{2,1,0:T(8,128)(2,1)S(1)}, bf16[1,192,1536]{2,1,0:T(8,128)(2,1)}, u32[]{:S(2)}) copy-start(bf16[1,192,1536]{2,1,0:T(8,128)(2,1)} %param.3) | copy-start | bytes 1769476
  7.2 115.2 %all-gather.14.cloned.1.call-start = ((), (), s32[]{:S(2)}) async-start(), calls=%async_computation.6 | async-start | bytes 5013504 | tf_op jit(solution)/shard_map/all_gather | solution.py:66
  7.9 180.6 %all-gather.8.cloned.1.call-start = ((), (), s32[]{:S(2)}) async-start(), calls=%async_computation.2 | async-start | bytes 5013504 | tf_op jit(solution)/shard_map/all_gather | solution.py:30
  106.5 2.8 copy-start.1
  106.5 5.2 copy-start.2
  110.3 143.3 %all-gather.10.cloned.1.call-start = ((), (), s32[]{:S(2)}) async-start(), calls=%async_computation.3 | async-start | bytes 5013504 | tf_op jit(solution)/shard_map/all_gather | solution.py:29
  111.1 226.8 %all-gather.12.cloned.1.call-start = ((), (), s32[]{:S(2)}) async-start(), calls=%async_computation.4 | async-start | bytes 5013504 | tf_op jit(solution)/shard_map/all_gather | solution.py:65
  111.7 378.6 %reduce-scatter.4.cloned.1.call-start = ((), (), s32[]{:S(2)}) async-start(), calls=%async_computation.7 | async-start | bytes 7520256
  253.7 23.8 %slice-start = ((s8[4718592]{0:T(1024)(128)(4,1)}), s8[524288]{0:T(1024)(128)(4,1)S(1)}, s32[]{:S(2)}) async-start(s8[4718592]{0:T(1024)(128)(4,1)} %bitcast.104), calls=%async_computation.8 | async-start | bytes 1048576
  260.4 17.1 %slice-start.1 = ((s8[4718592]{0:T(1024)(128)(4,1)}), s8[4194304]{0:T(1024)(128)(4,1)S(1)}, s32[]{:S(2)}) async-start(s8[4718592]{0:T(1024)(128)(4,1)} %bitcast.104), calls=%async_computation.9 | async-start | bytes 8388608
  327.1 26.9 %copy-start.4 = (f32[3072,6]{0,1:T(8,128)}, f32[3072,6]{0,1:T(8,128)S(1)}, u32[]{:S(2)}) copy-start(f32[3072,6]{0,1:T(8,128)S(1)} %reshape.65) | copy-start | bytes 221188
  388.6 1.0 copy-start.3
  388.6 239.5 %all-reduce.2.cloned.1.call-start = ((), (), s32[]{:S(2)}) async-start(), calls=%async_computation.5 | async-start | bytes 1179648 | tf_op jit(solution)/shard_map/psum | solution.py:112
Sparse Core Ops, SparseCore 0:
  10.7 111.5 all-gather.13
  125.6 62.8 all-gather.7
  191.8 61.8 all-gather.9
  256.8 62.3 all-gather.11
  388.8 101.4 reduce-scatter.3
  492.8 135.3 all-reduce.1
